TPU v7x, 256 devices: a whole 4x4x8 slice. The times are simulated.
256 devices in a mesh: pool: 8 (over y, core), group: 32 (over z, x).
Axes of the slice: x: 4, y: 4, z: 8, core: 2. Of those that a mesh axis runs over, the one named last changes fastest.
Arguments:
- queries: bfloat16 [32, 4, 8192], P('group', None, 'pool'), may hold values from -5.6 to 5.6
- new_keys: bfloat16 [32, 4, 1024], P('group', None, 'pool'), may hold values from -6 to 6
- new_values: bfloat16 [32, 4, 1024], P('group', None, 'pool'), may hold values from -8 to 8
- key_cache: bfloat16 [1024, 512, 1024], P('group', None, 'pool'), may hold values from -34 to 34
- value_cache: bfloat16 [1024, 512, 1024], P('group', None, 'pool'), may hold values from -8 to 8
- lengths: int32 [32], replicated, may hold values from 1 to 16384, as said below
- slot_request: int32 [1024], P('group'), may hold values from 0 to 31
- slot_block: int32 [1024], P('group'), may hold values from 0 to 32, as said below
- out_weight: bfloat16 [8192, 8192], P('pool', 'group'), may hold values from -0.0625 to 0.0625
Outputs:
- projected: bfloat16 [128, 8192], P('pool', 'group')
Inputs may be any that keep to these rules, and one draw needn't show every extreme that they name: `lengths`: some request has exactly 16384 cached tokens. `slot_block`: block b of a request holds its tokens b * 512 to b * 512 + 511. Each block b with b * 512 < lengths[r] of each request r sits in exactly one slot; every other slot has block number 32 and holds no tokens.
All inputs are finite; a program needn't handle non-finite values.
Results may differ from a plain program's by a relative error of at most 0.0052.
Values may be sent and summed in bfloat16 or wider, within the bound.
A program may use at most 64 MiB of HBM per device.

v0:
```python
import math

import jax
import jax.numpy as jnp
from jax import lax
from jax.sharding import PartitionSpec as P

HD = 128
STEPS = 4
GQA = 8


masked_score = -1e30


def slot_terms(panel_rows, key_rows, value_rows, live_count):
    slot_count = key_rows.shape[0]
    block_width = key_rows.shape[1]
    kv_heads = key_rows.shape[2] // HD
    query_heads = panel_rows.reshape(slot_count, STEPS, kv_heads, GQA, HD)
    key_heads = key_rows.reshape(slot_count, block_width, kv_heads, HD)
    scores = jnp.einsum(
        "sikgd,stkd->sikgt", query_heads, key_heads, preferred_element_type=jnp.float32
    ) * (1.0 / math.sqrt(HD))
    live_mask = (jnp.arange(block_width)[None, :] < live_count[:, None])[:, None, None, None, :]
    scores = jnp.where(live_mask, scores, masked_score)
    slot_top = jnp.max(scores, axis=-1)
    weights = jnp.where(live_mask, jnp.exp(scores - slot_top[..., None]), 0.0)
    slot_total = jnp.sum(weights, axis=-1)
    value_heads = value_rows.reshape(slot_count, block_width, kv_heads, HD)
    slot_out = jnp.einsum(
        "sikgt,stkd->sikgd",
        weights.astype(jnp.bfloat16),
        value_heads,
        preferred_element_type=jnp.float32,
    )
    return (slot_top, slot_total, slot_out)


def new_terms(query_rows, key_rows, value_rows):
    request_count = query_rows.shape[0]
    kv_heads = key_rows.shape[2] // HD
    query_heads = query_rows.reshape(request_count, STEPS, kv_heads, GQA, HD)
    key_heads = key_rows.reshape(request_count, STEPS, kv_heads, HD)
    scores = jnp.einsum(
        "rikgd,rjkd->rikgj", query_heads, key_heads, preferred_element_type=jnp.float32
    ) * (1.0 / math.sqrt(HD))
    causal = (jnp.arange(STEPS)[:, None] >= jnp.arange(STEPS)[None, :])[None, :, None, None, :]
    scores = jnp.where(causal, scores, masked_score)
    new_top = jnp.max(scores, axis=-1)
    weights = jnp.where(causal, jnp.exp(scores - new_top[..., None]), 0.0)
    new_total = jnp.sum(weights, axis=-1)
    value_heads = value_rows.reshape(request_count, STEPS, kv_heads, HD)
    new_out = jnp.einsum(
        "rikgj,rjkd->rikgd",
        weights.astype(jnp.bfloat16),
        value_heads,
        preferred_element_type=jnp.float32,
    )
    return (new_top, new_total, new_out)


def combine(earlier, later):
    joint_top = jnp.maximum(earlier[0], later[0])
    early_scale = jnp.exp(earlier[0] - joint_top)
    late_scale = jnp.exp(later[0] - joint_top)
    return (
        joint_top,
        earlier[1] * early_scale + later[1] * late_scale,
        earlier[2] * early_scale[..., None] + later[2] * late_scale[..., None],
    )


def fold_slots(tables, slot_top, slot_total, slot_out, owner_hot):
    slot_count = owner_hot.shape[0]
    request_count = owner_hot.shape[1]
    matches = owner_hot[:, :, None, None, None] > 0.5
    slot_best = jnp.max(jnp.where(matches, slot_top[:, None], masked_score), axis=0)
    joint_top = jnp.maximum(tables[0], slot_best)
    top_at = jnp.dot(
        owner_hot, joint_top.reshape(request_count, -1), precision=lax.Precision.HIGHEST
    ).reshape(slot_top.shape)
    rescale = jnp.exp(slot_top - top_at)
    added_total = jnp.dot(
        owner_hot.T, (rescale * slot_total).reshape(slot_count, -1), precision=lax.Precision.HIGHEST
    )
    added_out = jnp.dot(
        owner_hot.T,
        (rescale[..., None] * slot_out).reshape(slot_count, -1),
        precision=lax.Precision.HIGHEST,
    )
    return (joint_top, added_total.reshape(tables[1].shape), added_out.reshape(tables[2].shape))


def finish(tables):
    request_count = tables[1].shape[0]
    ratio = tables[2] / tables[1][..., None]
    return ratio.astype(jnp.bfloat16).reshape(request_count * STEPS, -1)


def body(
    queries,
    new_keys,
    new_values,
    key_cache,
    value_cache,
    lengths,
    slot_request,
    slot_block,
    out_weight,
):
    panels = lax.all_gather(queries, "group", axis=0, tiled=True)
    total_requests = panels.shape[0]
    block_width = key_cache.shape[1]
    kv_heads = key_cache.shape[2] // HD
    live_count = jnp.clip(
        jnp.take(lengths, slot_request) - slot_block * block_width, 0, block_width
    )
    owner_hot = (slot_request[:, None] == jnp.arange(total_requests)[None, :]).astype(jnp.float32)
    stat_shape = (total_requests, STEPS, kv_heads, GQA)
    tables = (
        jnp.full(stat_shape, masked_score, jnp.float32),
        jnp.zeros(stat_shape, jnp.float32),
        jnp.zeros(stat_shape + (HD,), jnp.float32),
    )
    panel_rows = jnp.take(panels, slot_request, axis=0)
    slot_top, slot_total, slot_out = slot_terms(panel_rows, key_cache, value_cache, live_count)
    tables = fold_slots(tables, slot_top, slot_total, slot_out, owner_hot)
    local_terms = new_terms(queries, new_keys, new_values)
    received = (
        lax.all_to_all(tables[0][None], "group", split_axis=1, concat_axis=0, tiled=True),
        lax.all_to_all(tables[1][None], "group", split_axis=1, concat_axis=0, tiled=True),
        lax.all_to_all(tables[2][None], "group", split_axis=1, concat_axis=0, tiled=True),
    )
    joint_top = jnp.max(received[0], axis=0)
    rescale = jnp.exp(received[0] - joint_top[None])
    holder_terms = (
        joint_top,
        jnp.sum(rescale * received[1], axis=0),
        jnp.sum(rescale[..., None] * received[2], axis=0),
    )
    own_terms = combine(holder_terms, local_terms)
    attention = lax.all_gather(finish(own_terms), "group", axis=0, tiled=True)
    projected = lax.psum_scatter(
        jnp.dot(attention, out_weight, preferred_element_type=jnp.float32),
        "pool",
        scatter_dimension=0,
        tiled=True,
    )
    return projected.astype(jnp.bfloat16)


def solution(mesh):
    in_specs = (
        P("group", None, "pool"),
        P("group", None, "pool"),
        P("group", None, "pool"),
        P("group", None, "pool"),
        P("group", None, "pool"),
        P(),
        P("group"),
        P("group"),
        P("pool", "group"),
    )
    out_specs = P("pool", "group")
    return jax.shard_map(body, mesh=mesh, in_specs=in_specs, out_specs=out_specs, check_vma=False)
```

profile of v0, /device:TPU:1, one launch (start us, length us, event | category | flops | bytes accessed | tf_op | source)
XLA Modules:
  0.0 203.7 jit_solution(7530752997885162420)
XLA Ops:
  6.5 0.7 compare_select_fusion
  7.3 0.7 convert_compare_fusion
  8.0 1.4 gather_fusion
  9.3 0.7 subtract_clamp_fusion
  10.1 40.8 %all_gather.6 = bf16[32,4,1024]{2,1,0:T(4,128)(2,1)S(1)} all-gather(bf16[1,4,1024]{2,1,0:T(4,128)(2,1)} %param.9), channel_id=1, replica_groups=mesh['pool'=8,'group'=32] {'group'}, dimensions={0}, use_global_device_ids=true | all-gather | bytes 270336 | tf_op jit(solution)/shard_map/all_gather | solution.py:112
  51.0 0.8 gather_fusion.1
  51.7 0.1 gather.12
  51.9 3.9 %fusion.5 = (f32[32,4,8]{2,1,0:T(4,128)S(1)}, f32[32,4,8,512]{3,2,1,0:T(8,128)S(1)}) fusion(pred[32,512]{1,0:T(8,128)(4,1)S(1)} %iota_compare_fusion, bf16[32,512,128]{2,1,0:T(8,128)(2,1)} %param.12, bf16[32,4,8,128]{3,2,1,0:T(8,128)(2,1)S(1)} %gather.12, pred[32]{0:T(512)(128)(4,1)S(1)} %get-tuple-element.9), kind=kOutput, calls=%fused_computation.9 | convolution fusion | flops 135920640 | bytes 6574112 | tf_op jit(solution)/shard_map/sikgd,stkd->sikgt/dot_general | solution.py:22
  55.8 1.0 fusion.6
  56.8 0.2 select_reduce_fusion
  57.1 0.2 fusion.17
  57.3 0.2 convolution_bitcast_fusion.2
  57.5 0.7 copy.52
  58.2 5.7 %all-to-all-start.2 = ((f32[1,32,4,1,8]{4,2,3,0,1:T(4,128)}), f32[1,32,4,1,8]{4,2,3,0,1:T(4,128)S(1)}, u32[]{:S(2)}, u32[]{:S(2)}) async-start(f32[1,32,4,1,8]{4,2,3,0,1:T(4,128)} %copy.52), calls=%async_computation.2 | async-start | bytes 131072 | tf_op jit(solution)/shard_map/all_to_all | solution.py:132
  64.1 3.3 %fusion.14 = f32[32,4,1,8,128]{4,3,1,0,2:T(8,128)S(1)} fusion(bf16[32,512,128]{2,1,0:T(8,128)(2,1)} %param.13, f32[32,4,8,512]{3,2,1,0:T(8,128)S(1)} %get-tuple-element.13, f32[32,4,8]{2,1,0:T(4,128)S(1)} %get-tuple-element.12, pred[32,512]{1,0:T(8,128)(4,1)S(1)} %iota_compare_fusion, f32[32,4,8]{2,1,0:T(4,128)S(1)} %copy.45), kind=kOutput, calls=%fused_computation.15 | convolution fusion | flops 136970240 | bytes 6840320 | tf_op jit(solution)/shard_map/sikgt,stkd->sikgd/dot_general | solution.py:31
  67.4 0.1 convolution_multiply_fusion
  67.5 0.7 copy.43
  68.3 0.1 reshape.309
  68.4 0.1 copy.57
  68.5 4.3 %all-to-all-done.2 = f32[1,32,4,1,8]{4,2,3,0,1:T(4,128)S(1)} async-done(((f32[1,32,4,1,8]{4,2,3,0,1:T(4,128)}), f32[1,32,4,1,8]{4,2,3,0,1:T(4,128)S(1)}, u32[]{:S(2)}, u32[]{:S(2)}) %all-to-all-start.2) | async-done | bytes 4128 | tf_op jit(solution)/shard_map/all_to_all | solution.py:132
  72.7 5.0 %all-to-all-start = ((f32[1,32,4,1,8]{4,2,3,0,1:T(4,128)}), f32[1,32,4,1,8]{4,2,3,0,1:T(4,128)S(1)}, u32[]{:S(2)}, u32[]{:S(2)}) async-start(f32[1,32,4,1,8]{4,2,3,0,1:T(4,128)} %copy.43), calls=%async_computation | async-start | bytes 131072 | tf_op jit(solution)/shard_map/all_to_all | solution.py:131
  77.7 0.7 convolution_bitcast_fusion
  78.5 1.1 copy.48
  79.6 7.7 %all-to-all-done = f32[1,32,4,1,8]{4,2,3,0,1:T(4,128)S(1)} async-done(((f32[1,32,4,1,8]{4,2,3,0,1:T(4,128)}), f32[1,32,4,1,8]{4,2,3,0,1:T(4,128)S(1)}, u32[]{:S(2)}, u32[]{:S(2)}) %all-to-all-start) | async-done | bytes 4128 | tf_op jit(solution)/shard_map/all_to_all | solution.py:131
  87.3 3.9 %all-to-all-start.1 = ((f32[1,32,4,1,8,128]{5,4,2,3,0,1:T(8,128)}), f32[1,32,4,1,8,128]{5,4,2,3,0,1:T(8,128)S(1)}, u32[]{:S(2)}, u32[]{:S(2)}) async-start(f32[1,32,4,1,8,128]{5,4,2,3,0,1:T(8,128)} %copy.48), calls=%async_computation.1 | async-start | bytes 1048576 | tf_op jit(solution)/shard_map/all_to_all | solution.py:133
  91.6 13.3 %all-to-all-done.1 = f32[1,32,4,1,8,128]{5,4,2,3,0,1:T(8,128)S(1)} async-done(((f32[1,32,4,1,8,128]{5,4,2,3,0,1:T(8,128)}), f32[1,32,4,1,8,128]{5,4,2,3,0,1:T(8,128)S(1)}, u32[]{:S(2)}, u32[]{:S(2)}) %all-to-all-start.1) | async-done | bytes 524320 | tf_op jit(solution)/shard_map/all_to_all | solution.py:133
  104.8 0.2 fusion.31
  105.1 0.2 fusion.22
  105.3 37.2 %all-gather = bf16[32,4,1024]{2,1,0:T(4,128)(2,1)S(1)} all-gather(bf16[1,4,1024]{2,1,0:T(4,128)(2,1)S(1)} %reshape.336), channel_id=1, replica_groups=mesh['pool'=8,'group'=32] {'group'}, dimensions={0}, use_global_device_ids=true | all-gather | bytes 270336 | tf_op jit(solution)/shard_map/all_gather | solution.py:143
  142.5 0.9 fusion.70
  143.4 52.1 %reduce-scatter.2.cloned.1.call-done = f32[16,256]{1,0:T(8,128)} async-done(((f32[128,256]{1,0:T(8,128)}), f32[16,256]{1,0:T(8,128)}) %reduce-scatter.2.cloned.1.call-update) | async-done | bytes 16400 | tf_op jit(solution)/shard_map/reduce_scatter | solution.py:144
  195.5 1.3 convert_element_type.23
  (27 shorter events, 0.8 us)
Async XLA Ops:
  6.5 136.0 %copy-start = (bf16[1024,256]{1,0:T(8,128)(2,1)S(1)}, bf16[1024,256]{1,0:T(8,128)(2,1)}, u32[]{:S(2)}) copy-start(bf16[1024,256]{1,0:T(8,128)(2,1)} %param.17) | copy-start | bytes 1572868
  55.7 1.3 copy-start.2
  58.2 14.5 %all-to-all-start.2 = ((f32[1,32,4,1,8]{4,2,3,0,1:T(4,128)}), f32[1,32,4,1,8]{4,2,3,0,1:T(4,128)S(1)}, u32[]{:S(2)}, u32[]{:S(2)}) async-start(f32[1,32,4,1,8]{4,2,3,0,1:T(4,128)} %copy.52), calls=%async_computation.2 | async-start | bytes 131072 | tf_op jit(solution)/shard_map/all_to_all | solution.py:132
  64.0 3.4 %copy-start.1 = (bf16[1,4,1024]{2,1,0:T(4,128)(2,1)S(1)}, bf16[1,4,1024]{2,1,0:T(4,128)(2,1)}, u32[]{:S(2)}) copy-start(bf16[1,4,1024]{2,1,0:T(4,128)(2,1)} %param.9) | copy-start | bytes 24580
  64.0 3.4 %copy-start.3 = (bf16[1,4,128]{2,1,0:T(4,128)(2,1)S(1)}, bf16[1,4,128]{2,1,0:T(4,128)(2,1)}, u32[]{:S(2)}) copy-start(bf16[1,4,128]{2,1,0:T(4,128)(2,1)} %param.10) | copy-start | bytes 3076
  72.7 14.6 %all-to-all-start = ((f32[1,32,4,1,8]{4,2,3,0,1:T(4,128)}), f32[1,32,4,1,8]{4,2,3,0,1:T(4,128)S(1)}, u32[]{:S(2)}, u32[]{:S(2)}) async-start(f32[1,32,4,1,8]{4,2,3,0,1:T(4,128)} %copy.43), calls=%async_computation | async-start | bytes 131072 | tf_op jit(solution)/shard_map/all_to_all | solution.py:131
  77.7 27.3 %copy-start.4 = (bf16[1,4,128]{2,1,0:T(4,128)(2,1)S(1)}, bf16[1,4,128]{2,1,0:T(4,128)(2,1)}, u32[]{:S(2)}) copy-start(bf16[1,4,128]{2,1,0:T(4,128)(2,1)} %param.11) | copy-start | bytes 3076
  87.3 17.5 %all-to-all-start.1 = ((f32[1,32,4,1,8,128]{5,4,2,3,0,1:T(8,128)}), f32[1,32,4,1,8,128]{5,4,2,3,0,1:T(8,128)S(1)}, u32[]{:S(2)}, u32[]{:S(2)}) async-start(f32[1,32,4,1,8,128]{5,4,2,3,0,1:T(8,128)} %copy.48), calls=%async_computation.1 | async-start | bytes 1048576 | tf_op jit(solution)/shard_map/all_to_all | solution.py:133
  91.2 104.3 %reduce-scatter.2.cloned.1.call-start = ((), (), s32[]{:S(2)}) async-start(), calls=%async_computation.4 | async-start | bytes 147456 | tf_op jit(solution)/shard_map/reduce_scatter | solution.py:144
Sparse Core Ops, SparseCore 0:
  143.6 51.9 reduce-scatter.1
where the time goes:
time: 206 us; the launch traced here: 204 us
  blocking collectives  78 us (38%)
  waiting for transfers between devices  77.4 us (38%)
  starting transfers between devices  14.6 us (7%)
  between operations  13.6 us (7%)
  matrix products  9.51 us (5%)
  local copies, waits for them, and re-layouts  5.32 us (3%)
  other arithmetic  5.23 us (3%)
    reduce_scatter x1, waiting for transfers between devices, body(): lax.psum_scatter(jnp.dot(attention, out_weight, preferred_element_type=jn...  52.1 us
    all_gather x1, blocking collectives, body(): panels = lax.all_gather(queries, 'group', axis=0, tiled=True)  40.8 us
    all_gather x1, blocking collectives, body(): attention = lax.all_gather(finish(own_terms), 'group', axis=0, tiled=True)  37.2 us
    all_to_all x1, waiting for transfers between devices, body(): lax.all_to_all(tables[2][None], 'group', split_axis=1, concat_axis=0, til...  13.3 us
    all_to_all x1, waiting for transfers between devices, body(): lax.all_to_all(tables[0][None], 'group', split_axis=1, concat_axis=0, til...  7.72 us
    all_to_all x1, starting transfers between devices, body(): lax.all_to_all(tables[1][None], 'group', split_axis=1, concat_axis=0, til...  5.72 us
    all_to_all x1, starting transfers between devices, body(): lax.all_to_all(tables[0][None], 'group', split_axis=1, concat_axis=0, til...  4.96 us
    all_to_all x1, waiting for transfers between devices, body(): lax.all_to_all(tables[1][None], 'group', split_axis=1, concat_axis=0, til...  4.28 us
  transfers between devices with their start and end apart: 4, of which 4 were waited for; matrix products, arithmetic and copies ran while one was open for 3% of the time, Pallas kernels for 0%

commit v1 on v0

v1 whole, which is shorter than its diff:
```python
import functools
import math

import jax
import jax.numpy as jnp
from jax import lax
from jax.experimental import pallas as pl
from jax.experimental.pallas import tpu as pltpu
from jax.sharding import PartitionSpec as P

HD = 128
STEPS = 4
GQA = 8
ROWS = STEPS * GQA
NX = 4
NZ = 8

MESH = pl.DeviceIdType.MESH
masked_score = -1e30
floor_score = -1e29
log2e = math.log2(math.e)


def wait_bytes(ref, sem):
    pltpu.make_async_copy(ref, ref, sem).wait()


def kernel(
    q_ref,
    nk_ref,
    nv_ref,
    len_ref,
    sreq_ref,
    sblk_ref,
    k_hbm,
    v_hbm,
    w_hbm,
    o_ref,
    k_vm,
    v_vm,
    w_vm,
    q_f32,
    q_all,
    scores,
    tops,
    outs,
    table_f32,
    table,
    stats,
    got,
    got_stats,
    att_all,
    att_f32,
    y_f32,
    y_got,
    load_sem,
    send_sem,
    recv_sem,
):
    slots, block_width = k_vm.shape[0], k_vm.shape[1]
    requests = q_all.shape[0]
    pools = y_got.shape[0]
    g = lax.axis_index("group")
    p = lax.axis_index("pool")
    z, x = g // NX, g % NX
    scale = log2e / math.sqrt(HD)

    loads = [
        pltpu.make_async_copy(k_hbm, k_vm, load_sem.at[0]),
        pltpu.make_async_copy(v_hbm, v_vm, load_sem.at[1]),
        pltpu.make_async_copy(w_hbm, w_vm, load_sem.at[2]),
    ]
    for load in loads:
        load.start()

    offsets = [(dz, dx) for dz in (4, 3, 5, 2, 6, 1, 7, 0) for dx in (2, 1, 3, 0)]
    peers = [
        lax.rem(z + dz, NZ) * NX + lax.rem(x + dx, NX) for dz, dx in offsets if (dz, dx) != (0, 0)
    ]
    pool_peers = [lax.rem(p + d, pools) for d in (4, 5, 3, 2, 6, 7, 1)]

    barrier = pltpu.get_barrier_semaphore()
    for peer in peers:
        pl.semaphore_signal(barrier, inc=1, device_id={"group": peer}, device_id_type=MESH)
    for peer in pool_peers:
        pl.semaphore_signal(barrier, inc=1, device_id={"pool": peer}, device_id_type=MESH)

    q_rows = q_ref[0].astype(jnp.float32)
    for h in range(GQA):
        q_f32[pl.ds(h, STEPS, stride=GQA), :] = q_rows[:, h * HD : (h + 1) * HD]
    own_q = q_f32[...]
    q_all[g] = own_q.astype(jnp.bfloat16)

    pl.semaphore_wait(barrier, len(peers) + len(pool_peers))

    def to_group(src, dst, phase):
        for peer in peers:
            pltpu.make_async_remote_copy(
                src_ref=src(peer),
                dst_ref=dst,
                send_sem=send_sem.at[phase],
                recv_sem=recv_sem.at[phase],
                device_id={"group": peer},
                device_id_type=MESH,
            ).start()

    to_group(lambda peer: q_all.at[g], q_all.at[g], 0)

    row_step = lax.broadcasted_iota(jnp.int32, (ROWS, 1), 0) // GQA
    nk = nk_ref[0].astype(jnp.float32)
    nv = nv_ref[0].astype(jnp.float32)
    new_scores = []
    for j in range(STEPS):
        s = jnp.sum(own_q * nk[j : j + 1, :], axis=1, keepdims=True) * scale
        new_scores.append(jnp.where(row_step >= j, s, masked_score))
    new_top = functools.reduce(jnp.maximum, new_scores)
    new_total = jnp.zeros((ROWS, 1), jnp.float32)
    new_out = jnp.zeros((ROWS, HD), jnp.float32)
    for j in range(STEPS):
        w = jnp.exp2(new_scores[j] - new_top)
        new_total += w
        new_out += w.astype(jnp.bfloat16).astype(jnp.float32) * nv[j : j + 1, :]

    lane = lax.broadcasted_iota(jnp.int32, (ROWS, HD), 1)
    token = lax.broadcasted_iota(jnp.int32, (ROWS, block_width), 1)
    owner = jnp.full((ROWS, HD), -1, jnp.int32)
    for s in range(slots):
        owner = jnp.where(lane == s, sreq_ref[s], owner)

    loads[0].wait()
    others = pl.ds(0, len(peers))
    wait_bytes(q_all.at[others], recv_sem.at[0])

    unroll = 4

    def score_slots(it, top):
        for u in range(unroll):
            s = it * unroll + u
            r = sreq_ref[s]
            live = jnp.clip(len_ref[r] - sblk_ref[s] * block_width, 0, block_width)
            sc = lax.dot_general(
                q_all[r], k_vm[s], (((1,), (1,)), ((), ())), preferred_element_type=jnp.float32
            )
            sc = jnp.where(token < live, sc * scale, masked_score)
            scores[s] = sc
            top = jnp.where(lane == s, jnp.max(sc, axis=1, keepdims=True), top)
        return top

    top = lax.fori_loop(
        0, slots // unroll, score_slots, jnp.full((ROWS, HD), masked_score, jnp.float32)
    )

    request_top = jnp.full((ROWS, HD), masked_score, jnp.float32)
    for r in range(requests):
        m = jnp.max(jnp.where(owner == r, top, masked_score), axis=1, keepdims=True)
        request_top = jnp.where(lane == r, m, request_top)
        tops[r] = jnp.broadcast_to(jnp.maximum(m, floor_score), (ROWS, HD))

    loads[1].wait()

    def weigh_slots(it, total):
        for u in range(unroll):
            s = it * unroll + u
            m = tops[sreq_ref[s]]
            w = jnp.exp2(scores[s] - jnp.concatenate([m] * (block_width // HD), axis=1))
            total = jnp.where(lane == s, jnp.sum(w, axis=1, keepdims=True), total)
            out = jnp.dot(w.astype(jnp.bfloat16), v_vm[s], preferred_element_type=jnp.float32)
            outs[pl.ds(pl.multiple_of(s * ROWS, ROWS), ROWS), :] = out
        return total

    total = lax.fori_loop(
        0, slots // unroll, weigh_slots, jnp.zeros((ROWS, HD), jnp.float32)
    )

    hot = (lax.broadcasted_iota(jnp.int32, (ROWS, HD), 0) == owner).astype(jnp.float32)
    request_total = lax.dot_general(
        total,
        hot,
        (((1,), (1,)), ((), ())),
        precision=lax.Precision.HIGHEST,
        preferred_element_type=jnp.float32,
    )
    request_total = jnp.concatenate(
        [request_total, jnp.zeros((ROWS, HD - requests), jnp.float32)], axis=1
    )
    pair = jnp.concatenate(
        [request_top, request_total, jnp.zeros((HD - 2 * ROWS, HD), jnp.float32)], axis=0
    )
    stats[...] = pair.T[:requests].reshape(requests, 1, HD)
    hot_slots = hot[:, :slots].astype(jnp.bfloat16)
    hot_twice = jnp.concatenate([hot_slots, hot_slots], axis=1)
    for j in range(ROWS):
        o = outs[pl.ds(j, slots, stride=ROWS), :]
        high = o.astype(jnp.bfloat16)
        low = (o - high.astype(jnp.float32)).astype(jnp.bfloat16)
        table_f32[pl.ds(j, requests, stride=ROWS), :] = jnp.dot(
            hot_twice, jnp.concatenate([high, low], axis=0), preferred_element_type=jnp.float32
        )
    table[...] = table_f32[...].astype(jnp.bfloat16).reshape(requests, ROWS, HD)

    to_group(lambda peer: stats.at[peer], got_stats.at[g], 1)
    to_group(lambda peer: table.at[peer], got.at[g], 2)
    got[g] = table[g]
    got_stats[g] = stats[g]
    wait_bytes(got_stats.at[others], recv_sem.at[1])

    stat_rows = got_stats[...].reshape(requests, HD)
    turned = jnp.concatenate([stat_rows, jnp.zeros((HD - requests, HD), jnp.float32)], axis=0).T
    held_top = jnp.where(lane < requests, turned[:ROWS], masked_score)
    held_total = turned[ROWS : 2 * ROWS]
    best = jnp.maximum(jnp.max(held_top, axis=1, keepdims=True), new_top)
    held_scale = jnp.exp2(held_top - best)
    new_scale = jnp.exp2(new_top - best)
    denominator = new_scale * new_total + jnp.sum(held_scale * held_total, axis=1, keepdims=True)
    inverse = 1.0 / denominator
    wait_bytes(got.at[others], recv_sem.at[2])
    numerator = new_scale * new_out
    for h in range(requests):
        numerator += held_scale[:, h : h + 1] * got[h].astype(jnp.float32)
    att_all[g] = (numerator * inverse).astype(jnp.bfloat16)

    to_group(lambda peer: att_all.at[g], att_all.at[g], 3)
    loads[2].wait()
    wait_bytes(att_all.at[others], recv_sem.at[3])

    att_f32[...] = att_all[...].reshape(requests * ROWS, HD).astype(jnp.float32)
    att = jnp.concatenate(
        [
            att_f32[pl.ds(h, requests * STEPS, stride=GQA), :].astype(jnp.bfloat16)
            for h in range(GQA)
        ],
        axis=1,
    )
    y = jnp.dot(att, w_vm[...], preferred_element_type=jnp.float32)
    y_f32[...] = y.reshape(y_f32.shape)

    for peer in pool_peers:
        pltpu.make_async_remote_copy(
            src_ref=y_f32.at[peer],
            dst_ref=y_got.at[p],
            send_sem=send_sem.at[4],
            recv_sem=recv_sem.at[4],
            device_id={"pool": peer},
            device_id_type=MESH,
        ).start()
    wait_bytes(y_got.at[pl.ds(0, pools - 1)], recv_sem.at[4])
    result = y_f32[p]
    for peer in pool_peers:
        result += y_got[peer]
    o_ref[...] = result.astype(o_ref.dtype)

    wait_bytes(q_all.at[others], send_sem.at[0])
    wait_bytes(got_stats.at[others], send_sem.at[1])
    wait_bytes(got.at[others], send_sem.at[2])
    wait_bytes(att_all.at[others], send_sem.at[3])
    wait_bytes(y_got.at[pl.ds(0, pools - 1)], send_sem.at[4])


def body(
    queries,
    new_keys,
    new_values,
    key_cache,
    value_cache,
    lengths,
    slot_request,
    slot_block,
    out_weight,
):
    slots, block_width, _ = key_cache.shape
    requests = lengths.shape[0]
    columns = out_weight.shape[1]
    pools = lax.axis_size("pool")
    out_rows = requests * STEPS // pools
    vmem = pl.BlockSpec(memory_space=pltpu.VMEM)
    smem = pl.BlockSpec(memory_space=pltpu.SMEM)
    hbm = pl.BlockSpec(memory_space=pl.ANY)
    return pl.pallas_call(
        kernel,
        out_shape=jax.ShapeDtypeStruct((out_rows, columns), jnp.bfloat16),
        in_specs=[vmem, vmem, vmem, smem, smem, smem, hbm, hbm, hbm],
        out_specs=vmem,
        scratch_shapes=[
            pltpu.VMEM(key_cache.shape, jnp.bfloat16),
            pltpu.VMEM(value_cache.shape, jnp.bfloat16),
            pltpu.VMEM(out_weight.shape, jnp.bfloat16),
            pltpu.VMEM((ROWS, HD), jnp.float32),
            pltpu.VMEM((requests, ROWS, HD), jnp.bfloat16),
            pltpu.VMEM((slots, ROWS, block_width), jnp.float32),
            pltpu.VMEM((requests, ROWS, HD), jnp.float32),
            pltpu.VMEM((slots * ROWS, HD), jnp.float32),
            pltpu.VMEM((requests * ROWS, HD), jnp.float32),
            pltpu.VMEM((requests, ROWS, HD), jnp.bfloat16),
            pltpu.VMEM((requests, 1, HD), jnp.float32),
            pltpu.VMEM((requests, ROWS, HD), jnp.bfloat16),
            pltpu.VMEM((requests, 1, HD), jnp.float32),
            pltpu.VMEM((requests, ROWS, HD), jnp.bfloat16),
            pltpu.VMEM((requests * ROWS, HD), jnp.float32),
            pltpu.VMEM((pools, out_rows, columns), jnp.float32),
            pltpu.VMEM((pools, out_rows, columns), jnp.float32),
            pltpu.SemaphoreType.DMA((3,)),
            pltpu.SemaphoreType.DMA((5,)),
            pltpu.SemaphoreType.DMA((5,)),
        ],
        compiler_params=pltpu.CompilerParams(
            collective_id=0, has_side_effects=True, vmem_limit_bytes=48 << 20
        ),
        name="paged_attention",
    )(
        queries,
        new_keys,
        new_values,
        lengths,
        slot_request,
        slot_block,
        key_cache,
        value_cache,
        out_weight,
    )


def solution(mesh):
    in_specs = (
        P("group", None, "pool"),
        P("group", None, "pool"),
        P("group", None, "pool"),
        P("group", None, "pool"),
        P("group", None, "pool"),
        P(),
        P("group"),
        P("group"),
        P("pool", "group"),
    )
    out_specs = P("pool", "group")
    return jax.shard_map(body, mesh=mesh, in_specs=in_specs, out_specs=out_specs, check_vma=False)
```

time: 206 us -> 54.9 us (0.27)
  blocking collectives: 78 us -> 0 us
  waiting for transfers between devices: 77.4 us -> 0 us
  Pallas kernels: 0 us -> 46.7 us
  starting transfers between devices: 14.6 us -> 0 us
  between operations: 13.6 us -> 0.02 us
  matrix products: 9.51 us -> 0 us
  other arithmetic: 5.23 us -> 0 us
  local copies, waits for them, and re-layouts: 5.32 us -> 7.85 us
    all_gather x2 -> x0, blocking collectives: 78 us -> none  [the longest x1 40.8 us: body(): panels = lax.all_gather(queries, 'group', axis=0, tiled=True)]
    reduce_scatter x1 -> x0, waiting for transfers between devices: 52.1 us -> none  [body(): lax.psum_scatter(jnp.dot(attention, out_weight, preferred_element_type=jn...]
    pallas_call x0 -> x1, Pallas kernels: none -> 46.7 us  [body(): pl.pallas_call(kernel, out_shape=jax.ShapeDtypeStruct((out_rows, columns)...]
    all_to_all x3 -> x0, waiting for transfers between devices: 25.2 us -> none  [the longest x1 13.3 us: body(): lax.all_to_all(tables[2][None], 'group', split_axis=1, concat_axis=0, til...]
    all_to_all x3 -> x0, starting transfers between devices: 14.6 us -> none  [the longest x1 5.72 us: body(): lax.all_to_all(tables[1][None], 'group', split_axis=1, concat_axis=0, til...]
    dot_general x8 -> x0, matrix products: 9.51 us -> none  [the longest x1 3.86 us: slot_terms(): jnp.einsum('sikgd,stkd->sikgt', query_heads, key_heads, preferred_element...]
    unnamed x13 -> x17, local copies, waits for them, and re-layouts: 0.21 us -> 7.85 us
    gather x3 -> x0, local copies, waits for them, and re-layouts: 2.23 us -> none  [the longest x1 1.36 us: body(): jnp.take(lengths, slot_request) - slot_block * block_width]
  transfers between devices with their start and end apart: 4 -> 0, of which waited for: 4 -> 0; matrix products, arithmetic and copies ran while one was open for 3% -> 0% of each run, Pallas kernels for 0% -> 0%
where the time goes in v1:
time: 54.9 us; the launch traced here: 54.6 us
  Pallas kernels  46.7 us (85%)
  local copies, waits for them, and re-layouts  7.85 us (14%)
    pallas_call x1, Pallas kernels, body(): pl.pallas_call(kernel, out_shape=jax.ShapeDtypeStruct((out_rows, columns)...  46.7 us
    unnamed x17, local copies, waits for them, and re-layouts  7.85 us

profile of v1, /device:TPU:1, one launch (start us, length us, event | category | flops | bytes accessed | tf_op | source)
XLA Modules:
  0.0 54.6 jit_solution(2039144258997078452)
XLA Ops:
  0.0 0.0 copy-start
  0.0 2.2 %copy-done = bf16[32,512,128]{2,1,0:T(8,128)(2,1)S(1)} copy-done((bf16[32,512,128]{2,1,0:T(8,128)(2,1)S(1)}, bf16[32,512,128]{2,1,0:T(8,128)(2,1)}, u32[]{:S(2)}) %copy-start) | copy-done | bytes 4194328
  2.2 0.0 copy-start.1
  2.2 1.0 %copy-done.1 = bf16[1024,256]{1,0:T(8,128)(2,1)S(1)} copy-done((bf16[1024,256]{1,0:T(8,128)(2,1)S(1)}, bf16[1024,256]{1,0:T(8,128)(2,1)}, u32[]{:S(2)}) %copy-start.1) | copy-done | bytes 524312
  3.2 0.0 copy-start.2
  3.2 0.7 %copy-done.2 = bf16[1,4,1024]{2,1,0:T(4,128)(2,1)S(1)} copy-done((bf16[1,4,1024]{2,1,0:T(4,128)(2,1)S(1)}, bf16[1,4,1024]{2,1,0:T(4,128)(2,1)}, u32[]{:S(2)}) %copy-start.2) | copy-done | bytes 8216
  3.9 0.0 copy-start.3
  3.9 0.7 %copy-done.3 = bf16[1,4,128]{2,1,0:T(4,128)(2,1)S(1)} copy-done((bf16[1,4,128]{2,1,0:T(4,128)(2,1)S(1)}, bf16[1,4,128]{2,1,0:T(4,128)(2,1)}, u32[]{:S(2)}) %copy-start.3) | copy-done | bytes 1048
  4.6 0.0 copy-start.4
  4.6 0.7 %copy-done.4 = bf16[1,4,128]{2,1,0:T(4,128)(2,1)S(1)} copy-done((bf16[1,4,128]{2,1,0:T(4,128)(2,1)S(1)}, bf16[1,4,128]{2,1,0:T(4,128)(2,1)}, u32[]{:S(2)}) %copy-start.4) | copy-done | bytes 1048
  5.3 0.0 copy-start.5
  5.3 0.7 %copy-done.5 = s32[32]{0:T(128)S(1)} copy-done((s32[32]{0:T(128)S(1)}, s32[32]{0:T(128)}, u32[]{:S(2)}) %copy-start.5) | copy-done | bytes 152
  5.9 0.0 copy-start.6
  5.9 0.7 %copy-done.6 = s32[32]{0:T(128)S(1)} copy-done((s32[32]{0:T(128)S(1)}, s32[32]{0:T(128)}, u32[]{:S(2)}) %copy-start.6) | copy-done | bytes 152
  6.6 0.0 copy-start.7
  6.6 0.7 %copy-done.7 = s32[32]{0:T(128)S(1)} copy-done((s32[32]{0:T(128)S(1)}, s32[32]{0:T(128)}, u32[]{:S(2)}) %copy-start.7) | copy-done | bytes 152
  7.3 46.7 %paged_attention.1 = bf16[16,256]{1,0:T(8,128)(2,1)S(1)} custom-call(bf16[1,4,1024]{2,1,0:T(4,128)(2,1)S(1)} %copy-done.2, bf16[1,4,128]{2,1,0:T(4,128)(2,1)S(1)} %copy-done.3, bf16[1,4,128]{2,1,0:T(4,128)(2,1)S(1)} %copy-done.4, s32[32]{0:T(128)S(1)} %copy-done.5, s32[32]{0:T(128)S(1)} %copy-done.6, s32[32]{0:T(128)S(1)} %copy-done.7, ...), custom_call_target="tpu_custom_call" | custom-call | tf_op jit(solution)/shard_map/paged_attention/pallas_call | solution.py:278
  54.0 0.6 %copy.11 = bf16[16,256]{1,0:T(8,128)(2,1)} copy(bf16[16,256]{1,0:T(8,128)(2,1)S(1)} %paged_attention.1) | data formatting | bytes 16384
Async XLA Ops:
  0.0 2.2 %copy-start = (bf16[32,512,128]{2,1,0:T(8,128)(2,1)S(1)}, bf16[32,512,128]{2,1,0:T(8,128)(2,1)}, u32[]{:S(2)}) copy-start(bf16[32,512,128]{2,1,0:T(8,128)(2,1)} %k_hbm.1) | copy-start | bytes 12582916
  2.2 1.0 %copy-start.1 = (bf16[1024,256]{1,0:T(8,128)(2,1)S(1)}, bf16[1024,256]{1,0:T(8,128)(2,1)}, u32[]{:S(2)}) copy-start(bf16[1024,256]{1,0:T(8,128)(2,1)} %w_hbm.1) | copy-start | bytes 1572868
  3.2 0.7 %copy-start.2 = (bf16[1,4,1024]{2,1,0:T(4,128)(2,1)S(1)}, bf16[1,4,1024]{2,1,0:T(4,128)(2,1)}, u32[]{:S(2)}) copy-start(bf16[1,4,1024]{2,1,0:T(4,128)(2,1)} %q_ref.1) | copy-start | bytes 24580
  3.9 0.7 %copy-start.3 = (bf16[1,4,128]{2,1,0:T(4,128)(2,1)S(1)}, bf16[1,4,128]{2,1,0:T(4,128)(2,1)}, u32[]{:S(2)}) copy-start(bf16[1,4,128]{2,1,0:T(4,128)(2,1)} %nk_ref.1) | copy-start | bytes 3076
  4.6 0.7 %copy-start.4 = (bf16[1,4,128]{2,1,0:T(4,128)(2,1)S(1)}, bf16[1,4,128]{2,1,0:T(4,128)(2,1)}, u32[]{:S(2)}) copy-start(bf16[1,4,128]{2,1,0:T(4,128)(2,1)} %nv_ref.1) | copy-start | bytes 3076
  5.3 0.7 %copy-start.5 = (s32[32]{0:T(128)S(1)}, s32[32]{0:T(128)}, u32[]{:S(2)}) copy-start(s32[32]{0:T(128)} %len_ref.1) | copy-start | bytes 388
  5.9 0.7 %copy-start.6 = (s32[32]{0:T(128)S(1)}, s32[32]{0:T(128)}, u32[]{:S(2)}) copy-start(s32[32]{0:T(128)} %sreq_ref.1) | copy-start | bytes 388
  6.6 0.7 %copy-start.7 = (s32[32]{0:T(128)S(1)}, s32[32]{0:T(128)}, u32[]{:S(2)}) copy-start(s32[32]{0:T(128)} %sblk_ref.1) | copy-start | bytes 388

commit v2 on v1

--- a/solution.py
+++ b/solution.py
@@ -26,12 +26,12 @@
 
 
 def kernel(
-    q_ref,
-    nk_ref,
-    nv_ref,
-    len_ref,
-    sreq_ref,
-    sblk_ref,
+    q_hbm,
+    nk_hbm,
+    nv_hbm,
+    len_hbm,
+    sreq_hbm,
+    sblk_hbm,
     k_hbm,
     v_hbm,
     w_hbm,
@@ -53,6 +53,12 @@
     att_f32,
     y_f32,
     y_got,
+    q_in,
+    nk_in,
+    nv_in,
+    len_in,
+    sreq_in,
+    sblk_in,
     load_sem,
     send_sem,
     recv_sem,
@@ -69,8 +75,14 @@
         pltpu.make_async_copy(k_hbm, k_vm, load_sem.at[0]),
         pltpu.make_async_copy(v_hbm, v_vm, load_sem.at[1]),
         pltpu.make_async_copy(w_hbm, w_vm, load_sem.at[2]),
+        pltpu.make_async_copy(q_hbm, q_in, load_sem.at[3]),
+        pltpu.make_async_copy(nk_hbm, nk_in, load_sem.at[4]),
+        pltpu.make_async_copy(nv_hbm, nv_in, load_sem.at[5]),
+        pltpu.make_async_copy(len_hbm, len_in, load_sem.at[6]),
+        pltpu.make_async_copy(sreq_hbm, sreq_in, load_sem.at[7]),
+        pltpu.make_async_copy(sblk_hbm, sblk_in, load_sem.at[8]),
     ]
-    for load in loads:
+    for load in loads[3:] + loads[:3]:
         load.start()
 
     offsets = [(dz, dx) for dz in (4, 3, 5, 2, 6, 1, 7, 0) for dx in (2, 1, 3, 0)]
@@ -85,7 +97,8 @@
     for peer in pool_peers:
         pl.semaphore_signal(barrier, inc=1, device_id={"pool": peer}, device_id_type=MESH)
 
-    q_rows = q_ref[0].astype(jnp.float32)
+    loads[3].wait()
+    q_rows = q_in[0].astype(jnp.float32)
     for h in range(GQA):
         q_f32[pl.ds(h, STEPS, stride=GQA), :] = q_rows[:, h * HD : (h + 1) * HD]
     own_q = q_f32[...]
@@ -107,8 +120,10 @@
     to_group(lambda peer: q_all.at[g], q_all.at[g], 0)
 
     row_step = lax.broadcasted_iota(jnp.int32, (ROWS, 1), 0) // GQA
-    nk = nk_ref[0].astype(jnp.float32)
-    nv = nv_ref[0].astype(jnp.float32)
+    for load in loads[4:]:
+        load.wait()
+    nk = nk_in[0].astype(jnp.float32)
+    nv = nv_in[0].astype(jnp.float32)
     new_scores = []
     for j in range(STEPS):
         s = jnp.sum(own_q * nk[j : j + 1, :], axis=1, keepdims=True) * scale
@@ -125,19 +140,19 @@
     token = lax.broadcasted_iota(jnp.int32, (ROWS, block_width), 1)
     owner = jnp.full((ROWS, HD), -1, jnp.int32)
     for s in range(slots):
-        owner = jnp.where(lane == s, sreq_ref[s], owner)
+        owner = jnp.where(lane == s, sreq_in[s], owner)
 
     loads[0].wait()
     others = pl.ds(0, len(peers))
     wait_bytes(q_all.at[others], recv_sem.at[0])
 
-    unroll = 4
+    unroll = 16
 
     def score_slots(it, top):
         for u in range(unroll):
             s = it * unroll + u
-            r = sreq_ref[s]
-            live = jnp.clip(len_ref[r] - sblk_ref[s] * block_width, 0, block_width)
+            r = sreq_in[s]
+            live = jnp.clip(len_in[r] - sblk_in[s] * block_width, 0, block_width)
             sc = lax.dot_general(
                 q_all[r], k_vm[s], (((1,), (1,)), ((), ())), preferred_element_type=jnp.float32
             )
@@ -161,7 +176,7 @@
     def weigh_slots(it, total):
         for u in range(unroll):
             s = it * unroll + u
-            m = tops[sreq_ref[s]]
+            m = tops[sreq_in[s]]
             w = jnp.exp2(scores[s] - jnp.concatenate([m] * (block_width // HD), axis=1))
             total = jnp.where(lane == s, jnp.sum(w, axis=1, keepdims=True), total)
             out = jnp.dot(w.astype(jnp.bfloat16), v_vm[s], preferred_element_type=jnp.float32)
@@ -273,12 +288,12 @@
     pools = lax.axis_size("pool")
     out_rows = requests * STEPS // pools
     vmem = pl.BlockSpec(memory_space=pltpu.VMEM)
-    smem = pl.BlockSpec(memory_space=pltpu.SMEM)
-    hbm = pl.BlockSpec(memory_space=pl.ANY)
+    hbm = pl.BlockSpec(memory_space=pltpu.HBM)
+    pin = lambda a: pltpu.with_memory_space_constraint(a, pltpu.HBM)
     return pl.pallas_call(
         kernel,
         out_shape=jax.ShapeDtypeStruct((out_rows, columns), jnp.bfloat16),
-        in_specs=[vmem, vmem, vmem, smem, smem, smem, hbm, hbm, hbm],
+        in_specs=[hbm] * 9,
         out_specs=vmem,
         scratch_shapes=[
             pltpu.VMEM(key_cache.shape, jnp.bfloat16),
@@ -298,7 +313,13 @@
             pltpu.VMEM((requests * ROWS, HD), jnp.float32),
             pltpu.VMEM((pools, out_rows, columns), jnp.float32),
             pltpu.VMEM((pools, out_rows, columns), jnp.float32),
-            pltpu.SemaphoreType.DMA((3,)),
+            pltpu.VMEM(queries.shape, jnp.bfloat16),
+            pltpu.VMEM(new_keys.shape, jnp.bfloat16),
+            pltpu.VMEM(new_values.shape, jnp.bfloat16),
+            pltpu.SMEM(lengths.shape, jnp.int32),
+            pltpu.SMEM(slot_request.shape, jnp.int32),
+            pltpu.SMEM(slot_block.shape, jnp.int32),
+            pltpu.SemaphoreType.DMA((9,)),
             pltpu.SemaphoreType.DMA((5,)),
             pltpu.SemaphoreType.DMA((5,)),
         ],
@@ -307,15 +328,15 @@
         ),
         name="paged_attention",
     )(
-        queries,
-        new_keys,
-        new_values,
-        lengths,
-        slot_request,
-        slot_block,
-        key_cache,
-        value_cache,
-        out_weight,
+        pin(queries),
+        pin(new_keys),
+        pin(new_values),
+        pin(lengths),
+        pin(slot_request),
+        pin(slot_block),
+        pin(key_cache),
+        pin(value_cache),
+        pin(out_weight),
     )
 
 

time: 54.9 us -> 44.9 us (0.82)
  local copies, waits for them, and re-layouts: 7.85 us -> 0.6 us
  Pallas kernels: 46.7 us -> 44.1 us
    unnamed x17 -> x1, local copies, waits for them, and re-layouts: 7.85 us -> 0.6 us
    pallas_call x1, Pallas kernels: 46.7 us -> 44.1 us  [body(): pl.pallas_call(kernel, out_shape=jax.ShapeDtypeStruct((out_rows, columns)...]
where the time goes in v2:
time: 44.9 us; the launch traced here: 44.7 us
  Pallas kernels  44.1 us (98%)
  local copies, waits for them, and re-layouts  0.6 us (1%)
    pallas_call x1, Pallas kernels, body(): pl.pallas_call(kernel, out_shape=jax.ShapeDtypeStruct((out_rows, columns)...  44.1 us

profile of v2, /device:TPU:1, one launch (start us, length us, event | category | flops | bytes accessed | tf_op | source)
XLA Modules:
  0.0 44.7 jit_solution(1551979833610163556)
XLA Ops:
  0.0 44.1 %paged_attention.1 = bf16[16,256]{1,0:T(8,128)(2,1)S(1)} custom-call(bf16[1,4,1024]{2,1,0:T(4,128)(2,1)} %q_hbm.1, bf16[1,4,128]{2,1,0:T(4,128)(2,1)} %nk_hbm.1, bf16[1,4,128]{2,1,0:T(4,128)(2,1)} %nv_hbm.1, s32[32]{0:T(128)} %len_hbm.1, s32[32]{0:T(128)} %sreq_hbm.1, s32[32]{0:T(128)} %sblk_hbm.1, bf16[32,512,128]{2,1,0:T(8,128)(2,1)} %k_hbm.1, ...), custom_call_target="tpu_custom_call" | custom-call | tf_op jit(solution)/shard_map/paged_attention/pallas_call | solution.py:293
  44.1 0.6 %copy.11 = bf16[16,256]{1,0:T(8,128)(2,1)} copy(bf16[16,256]{1,0:T(8,128)(2,1)S(1)} %paged_attention.1) | data formatting | bytes 16384

commit v3 on v2

v3 whole, which is shorter than its diff:
```python
import functools
import math

import jax
import jax.numpy as jnp
from jax import lax
from jax.experimental import pallas as pl
from jax.experimental.pallas import tpu as pltpu
from jax.sharding import PartitionSpec as P

HD = 128
STEPS = 4
GQA = 8
HALVES = 2
HEADS = GQA // HALVES
ROWS = STEPS * HEADS
BOTH = HALVES * ROWS
UNROLL = 32
TURNS = 4
NX = 4
NZ = 8

EVERY = [(dz, dx) for dz in (4, 3, 5, 2, 6, 1, 7, 0) for dx in (2, 1, 3, 0) if (dz, dx) != (0, 0)]
LINE_Z = (4, 3, 5, 2, 6, 1, 7)
LINE_X = (2, 1, 3)

MESH = pl.DeviceIdType.MESH
masked_score = -1e30
floor_score = -1e29
log2e = math.log2(math.e)


def wait_bytes(ref, sem):
    pltpu.make_async_copy(ref, ref, sem).wait()


def kernel(
    q_hbm,
    nk_hbm,
    nv_hbm,
    len_hbm,
    sreq_hbm,
    sblk_hbm,
    k_hbm,
    v_hbm,
    w_hbm,
    o_ref,
    k_vm,
    k_turned,
    v_vm,
    w_vm,
    q_f32,
    q_all,
    scores,
    tops,
    outs,
    table_f32,
    table,
    stats,
    got,
    got_stats,
    att_all,
    att_f32,
    y_f32,
    y_got,
    q_in,
    nk_in,
    nv_in,
    len_in,
    sreq_in,
    sblk_in,
    load_sem,
    send_sem,
    recv_sem,
    pool_sem,
    line_sem,
    query_sem,
):
    slots, block_width = k_vm.shape[0], k_vm.shape[1]
    requests = q_all.shape[0]
    pools = y_got.shape[0]
    g = lax.axis_index("group")
    p = lax.axis_index("pool")
    z, x = g // NX, g % NX
    scale = log2e / math.sqrt(HD)

    loads = [
        pltpu.make_async_copy(k_hbm, k_vm, load_sem.at[0]),
        pltpu.make_async_copy(v_hbm, v_vm, load_sem.at[1]),
        pltpu.make_async_copy(w_hbm, w_vm, load_sem.at[2]),
        pltpu.make_async_copy(q_hbm, q_in, load_sem.at[3]),
        pltpu.make_async_copy(nk_hbm, nk_in, load_sem.at[4]),
        pltpu.make_async_copy(nv_hbm, nv_in, load_sem.at[5]),
        pltpu.make_async_copy(len_hbm, len_in, load_sem.at[6]),
        pltpu.make_async_copy(sreq_hbm, sreq_in, load_sem.at[7]),
        pltpu.make_async_copy(sblk_hbm, sblk_in, load_sem.at[8]),
    ]
    for load in loads[3:] + loads[:3]:
        load.start()

    def peer_at(dz, dx):
        return lax.rem(z + dz, NZ) * NX + lax.rem(x + dx, NX)

    peers = [peer_at(dz, dx) for dz, dx in EVERY]
    others = pl.ds(0, len(peers))
    pool_peers = [lax.rem(p + d, pools) for d in (4, 5, 3, 2, 6, 7, 1)]

    barrier = pltpu.get_barrier_semaphore()
    for peer in [peer_at(dz, 0) for dz in LINE_Z] + [peer_at(0, dx) for dx in LINE_X]:
        pl.semaphore_signal(barrier, inc=1, device_id={"group": peer}, device_id_type=MESH)
    for peer in pool_peers:
        pl.semaphore_signal(barrier, inc=1, device_id={"pool": peer}, device_id_type=MESH)

    loads[3].wait()
    q_rows = q_in[0].astype(jnp.float32)
    for half in range(HALVES):
        for h in range(HEADS):
            at = (half * HEADS + h) * HD
            q_f32[pl.ds(half * ROWS + h, STEPS, stride=HEADS), :] = q_rows[:, at : at + HD]
    own_q = q_f32[...]
    q_all[g] = own_q.astype(jnp.bfloat16)

    pl.semaphore_wait(barrier, len(LINE_Z) + len(LINE_X) + len(pool_peers))

    def to_group(src, dst, phase, half):
        for peer in peers:
            pltpu.make_async_remote_copy(
                src_ref=src(peer),
                dst_ref=dst,
                send_sem=send_sem.at[phase, half],
                recv_sem=recv_sem.at[phase, half],
                device_id={"group": peer},
                device_id_type=MESH,
            ).start()

    def send_query(owner, target, sem):
        pltpu.make_async_remote_copy(
            src_ref=q_all.at[owner],
            dst_ref=q_all.at[owner],
            send_sem=query_sem.at[0],
            recv_sem=sem,
            device_id={"group": target},
            device_id_type=MESH,
        ).start()

    for dz in LINE_Z:
        send_query(g, peer_at(dz, 0), line_sem.at[dz])
    for dx in LINE_X:
        send_query(g, peer_at(0, dx), query_sem.at[1])

    for load in loads[4:]:
        load.wait()
    row_step = lax.broadcasted_iota(jnp.int32, (BOTH, 1), 0) % ROWS // HEADS
    nk = nk_in[0].astype(jnp.float32)
    nv = nv_in[0].astype(jnp.float32)
    new_scores = []
    for j in range(STEPS):
        s = jnp.sum(own_q * nk[j : j + 1, :], axis=1, keepdims=True) * scale
        new_scores.append(jnp.where(row_step >= j, s, masked_score))
    new_top = functools.reduce(jnp.maximum, new_scores)
    new_total = jnp.zeros((BOTH, 1), jnp.float32)
    new_out = jnp.zeros((BOTH, HD), jnp.float32)
    for j in range(STEPS):
        w = jnp.exp2(new_scores[j] - new_top)
        new_total += w
        new_out += w.astype(jnp.bfloat16).astype(jnp.float32) * nv[j : j + 1, :]

    lane = lax.broadcasted_iota(jnp.int32, (BOTH, HD), 1)
    half_lane = lane[:ROWS]
    token = lax.broadcasted_iota(jnp.int32, (BOTH, block_width), 1)
    owner = jnp.full((requests, HD), -1, jnp.int32)
    slot_lane = lax.broadcasted_iota(jnp.int32, (requests, HD), 1)
    for s in range(slots):
        owner = jnp.where(slot_lane == s, sreq_in[s], owner)
    hot = (lax.broadcasted_iota(jnp.int32, (requests, HD), 0) == owner).astype(jnp.float32)
    hot_slots = hot[:, :slots].astype(jnp.bfloat16)
    hot_twice = jnp.concatenate([hot_slots, hot_slots], axis=1)
    row_owner = owner[:BOTH]

    loads[0].wait()

    def turn_keys(it, carry):
        for u in range(TURNS):
            k_turned[it * TURNS + u] = k_vm[it * TURNS + u].T
        return carry

    lax.fori_loop(0, slots // TURNS, turn_keys, 0)
    loads[1].wait()

    for dz in LINE_Z[::-1]:
        block = peer_at(NZ - dz, 0)
        wait_bytes(q_all.at[block], line_sem.at[dz])
        for dx in LINE_X:
            send_query(block, peer_at(0, dx), query_sem.at[1])
    handed = NZ * len(LINE_X)
    wait_bytes(q_all.at[pl.ds(0, handed)], query_sem.at[1])

    def score_slots(it, top):
        for u in range(UNROLL):
            s = it * UNROLL + u
            r = sreq_in[s]
            live = jnp.clip(len_in[r] - sblk_in[s] * block_width, 0, block_width)
            sc = jnp.dot(q_all[r], k_turned[s], preferred_element_type=jnp.float32)
            sc = jnp.where(token < live, sc * scale, masked_score)
            scores[s] = sc
            top = jnp.where(lane == s, jnp.max(sc, axis=1, keepdims=True), top)
        return top

    top = lax.fori_loop(
        0, slots // UNROLL, score_slots, jnp.full((BOTH, HD), masked_score, jnp.float32)
    )

    request_top = jnp.full((BOTH, HD), masked_score, jnp.float32)
    for r in range(requests):
        m = jnp.max(jnp.where(row_owner == r, top, masked_score), axis=1, keepdims=True)
        request_top = jnp.where(lane == r, m, request_top)
        tops[r] = jnp.broadcast_to(jnp.maximum(m, floor_score), (BOTH, HD))

    def attend(half):
        rows = slice(half * ROWS, (half + 1) * ROWS)

        def weigh_slots(it, total):
            for u in range(UNROLL):
                s = it * UNROLL + u
                m = tops[sreq_in[s], rows, :]
                w = jnp.exp2(scores[s, rows, :] - jnp.concatenate([m] * (block_width // HD), axis=1))
                total = jnp.where(half_lane == s, jnp.sum(w, axis=1, keepdims=True), total)
                out = jnp.dot(w.astype(jnp.bfloat16), v_vm[s], preferred_element_type=jnp.float32)
                outs[pl.ds(pl.multiple_of(s * ROWS, ROWS), ROWS), :] = out
            return total

        total = lax.fori_loop(
            0, slots // UNROLL, weigh_slots, jnp.zeros((ROWS, HD), jnp.float32)
        )

        request_total = lax.dot_general(
            total,
            hot,
            (((1,), (1,)), ((), ())),
            precision=lax.Precision.HIGHEST,
            preferred_element_type=jnp.float32,
        )
        request_total = jnp.concatenate(
            [request_total, jnp.zeros((ROWS, HD - requests), jnp.float32)], axis=1
        )
        pair = jnp.concatenate(
            [request_top[rows], request_total, jnp.zeros((HD - 2 * ROWS, HD), jnp.float32)], axis=0
        )
        stats[half] = pair.T[:requests].reshape(requests, 1, HD)
        for j in range(ROWS):
            o = outs[pl.ds(j, slots, stride=ROWS), :]
            high = o.astype(jnp.bfloat16)
            low = (o - high.astype(jnp.float32)).astype(jnp.bfloat16)
            table_f32[pl.ds(j, requests, stride=ROWS), :] = jnp.dot(
                hot_twice, jnp.concatenate([high, low], axis=0), preferred_element_type=jnp.float32
            )
        table[half] = table_f32[...].astype(jnp.bfloat16).reshape(requests, ROWS, HD)

        to_group(lambda peer: stats.at[half, peer], got_stats.at[half, g], 0, half)
        to_group(lambda peer: table.at[half, peer], got.at[half, g], 1, half)
        got[half, g] = table[half, g]
        got_stats[half, g] = stats[half, g]

    for half in range(HALVES):
        attend(half)

    for half in range(HALVES):
        rows = slice(half * ROWS, (half + 1) * ROWS)
        own_top = new_top[rows]
        wait_bytes(got_stats.at[half, others], recv_sem.at[0, half])
        stat_rows = got_stats[half].reshape(requests, HD)
        turned = jnp.concatenate([stat_rows, jnp.zeros((HD - requests, HD), jnp.float32)], axis=0).T
        held_top = jnp.where(half_lane < requests, turned[:ROWS], masked_score)
        held_total = turned[ROWS : 2 * ROWS]
        best = jnp.maximum(jnp.max(held_top, axis=1, keepdims=True), own_top)
        held_scale = jnp.exp2(held_top - best)
        new_scale = jnp.exp2(own_top - best)
        denominator = new_scale * new_total[rows] + jnp.sum(
            held_scale * held_total, axis=1, keepdims=True
        )
        inverse = 1.0 / denominator
        held_scale = held_scale * inverse
        attention = new_scale * inverse * new_out[rows]
        wait_bytes(got.at[half, others], recv_sem.at[1, half])
        for h in range(requests):
            attention += held_scale[:, h : h + 1] * got[half, h].astype(jnp.float32)
        att_all[half, g] = attention.astype(jnp.bfloat16)
        mine = att_all.at[half, g]
        to_group(lambda peer: mine, mine, 2, half)

    loads[2].wait()
    y = jnp.zeros((requests * STEPS, w_vm.shape[1]), jnp.float32)
    for half in range(HALVES):
        wait_bytes(att_all.at[half, others], recv_sem.at[2, half])
        att_f32[...] = att_all[half].reshape(requests * ROWS, HD).astype(jnp.float32)
        att = jnp.concatenate(
            [
                att_f32[pl.ds(h, requests * STEPS, stride=HEADS), :].astype(jnp.bfloat16)
                for h in range(HEADS)
            ],
            axis=1,
        )
        rows = pl.ds(half * HEADS * HD, HEADS * HD)
        y += jnp.dot(att, w_vm[rows, :], preferred_element_type=jnp.float32)
    y_f32[...] = y.reshape(y_f32.shape)

    for peer in pool_peers:
        pltpu.make_async_remote_copy(
            src_ref=y_f32.at[peer],
            dst_ref=y_got.at[p],
            send_sem=pool_sem.at[0],
            recv_sem=pool_sem.at[1],
            device_id={"pool": peer},
            device_id_type=MESH,
        ).start()
    wait_bytes(y_got.at[pl.ds(0, pools - 1)], pool_sem.at[1])
    result = y_f32[p]
    for peer in pool_peers:
        result += y_got[peer]
    o_ref[...] = result.astype(o_ref.dtype)

    for half in range(HALVES):
        wait_bytes(got_stats.at[half, others], send_sem.at[0, half])
        wait_bytes(got.at[half, others], send_sem.at[1, half])
        wait_bytes(att_all.at[half, others], send_sem.at[2, half])
    wait_bytes(q_all.at[others], query_sem.at[0])
    wait_bytes(y_got.at[pl.ds(0, pools - 1)], pool_sem.at[0])


def body(
    queries,
    new_keys,
    new_values,
    key_cache,
    value_cache,
    lengths,
    slot_request,
    slot_block,
    out_weight,
):
    slots, block_width, _ = key_cache.shape
    requests = lengths.shape[0]
    columns = out_weight.shape[1]
    pools = lax.axis_size("pool")
    out_rows = requests * STEPS // pools
    vmem = pl.BlockSpec(memory_space=pltpu.VMEM)
    hbm = pl.BlockSpec(memory_space=pltpu.HBM)
    pin = lambda a: pltpu.with_memory_space_constraint(a, pltpu.HBM)
    return pl.pallas_call(
        kernel,
        out_shape=jax.ShapeDtypeStruct((out_rows, columns), jnp.bfloat16),
        in_specs=[hbm] * 9,
        out_specs=vmem,
        scratch_shapes=[
            pltpu.VMEM(key_cache.shape, jnp.bfloat16),
            pltpu.VMEM((slots, HD, block_width), jnp.bfloat16),
            pltpu.VMEM(value_cache.shape, jnp.bfloat16),
            pltpu.VMEM(out_weight.shape, jnp.bfloat16),
            pltpu.VMEM((BOTH, HD), jnp.float32),
            pltpu.VMEM((requests, BOTH, HD), jnp.bfloat16),
            pltpu.VMEM((slots, BOTH, block_width), jnp.float32),
            pltpu.VMEM((requests, BOTH, HD), jnp.float32),
            pltpu.VMEM((slots * ROWS, HD), jnp.float32),
            pltpu.VMEM((requests * ROWS, HD), jnp.float32),
            pltpu.VMEM((HALVES, requests, ROWS, HD), jnp.bfloat16),
            pltpu.VMEM((HALVES, requests, 1, HD), jnp.float32),
            pltpu.VMEM((HALVES, requests, ROWS, HD), jnp.bfloat16),
            pltpu.VMEM((HALVES, requests, 1, HD), jnp.float32),
            pltpu.VMEM((HALVES, requests, ROWS, HD), jnp.bfloat16),
            pltpu.VMEM((requests * ROWS, HD), jnp.float32),
            pltpu.VMEM((pools, out_rows, columns), jnp.float32),
            pltpu.VMEM((pools, out_rows, columns), jnp.float32),
            pltpu.VMEM(queries.shape, jnp.bfloat16),
            pltpu.VMEM(new_keys.shape, jnp.bfloat16),
            pltpu.VMEM(new_values.shape, jnp.bfloat16),
            pltpu.SMEM(lengths.shape, jnp.int32),
            pltpu.SMEM(slot_request.shape, jnp.int32),
            pltpu.SMEM(slot_block.shape, jnp.int32),
            pltpu.SemaphoreType.DMA((9,)),
            pltpu.SemaphoreType.DMA((3, HALVES)),
            pltpu.SemaphoreType.DMA((3, HALVES)),
            pltpu.SemaphoreType.DMA((2,)),
            pltpu.SemaphoreType.DMA((NZ,)),
            pltpu.SemaphoreType.DMA((2,)),
        ],
        compiler_params=pltpu.CompilerParams(
            collective_id=0, has_side_effects=True, vmem_limit_bytes=48 << 20
        ),
        name="paged_attention",
    )(
        pin(queries),
        pin(new_keys),
        pin(new_values),
        pin(lengths),
        pin(slot_request),
        pin(slot_block),
        pin(key_cache),
        pin(value_cache),
        pin(out_weight),
    )


def solution(mesh):
    in_specs = (
        P("group", None, "pool"),
        P("group", None, "pool"),
        P("group", None, "pool"),
        P("group", None, "pool"),
        P("group", None, "pool"),
        P(),
        P("group"),
        P("group"),
        P("pool", "group"),
    )
    out_specs = P("pool", "group")
    return jax.shard_map(body, mesh=mesh, in_specs=in_specs, out_specs=out_specs, check_vma=False)
```

time: 44.9 us -> 40.3 us (0.90)
  Pallas kernels: 44.1 us -> 39.6 us
    pallas_call x1, Pallas kernels: 44.1 us -> 39.6 us  [body(): pl.pallas_call(kernel, out_shape=jax.ShapeDtypeStruct((out_rows, columns)...]
where the time goes in v3:
time: 40.3 us; the launch traced here: 40.2 us
  Pallas kernels  39.6 us (98%)
  local copies, waits for them, and re-layouts  0.6 us (1%)
    pallas_call x1, Pallas kernels, body(): pl.pallas_call(kernel, out_shape=jax.ShapeDtypeStruct((out_rows, columns)...  39.6 us

profile of v3, /device:TPU:1, one launch (start us, length us, event | category | flops | bytes accessed | tf_op | source)
XLA Modules:
  0.0 40.2 jit_solution(16768902349185963016)
XLA Ops:
  0.0 39.6 %paged_attention.1 = bf16[16,256]{1,0:T(8,128)(2,1)S(1)} custom-call(bf16[1,4,1024]{2,1,0:T(4,128)(2,1)} %q_hbm.1, bf16[1,4,128]{2,1,0:T(4,128)(2,1)} %nk_hbm.1, bf16[1,4,128]{2,1,0:T(4,128)(2,1)} %nv_hbm.1, s32[32]{0:T(128)} %len_hbm.1, s32[32]{0:T(128)} %sreq_hbm.1, s32[32]{0:T(128)} %sblk_hbm.1, bf16[32,512,128]{2,1,0:T(8,128)(2,1)} %k_hbm.1, ...), custom_call_target="tpu_custom_call" | custom-call | tf_op jit(solution)/shard_map/paged_attention/pallas_call | solution.py:349
  39.6 0.6 %copy.11 = bf16[16,256]{1,0:T(8,128)(2,1)} copy(bf16[16,256]{1,0:T(8,128)(2,1)S(1)} %paged_attention.1) | data formatting | bytes 16384

commit v4 on v3

--- a/solution.py
+++ b/solution.py
@@ -23,6 +23,8 @@
 EVERY = [(dz, dx) for dz in (4, 3, 5, 2, 6, 1, 7, 0) for dx in (2, 1, 3, 0) if (dz, dx) != (0, 0)]
 LINE_Z = (4, 3, 5, 2, 6, 1, 7)
 LINE_X = (2, 1, 3)
+ROWS_NEAR = EVERY[::-1]
+ROW_ORDER = (0, 1, 7, 2, 6, 3, 5, 4)
 
 MESH = pl.DeviceIdType.MESH
 masked_score = -1e30
@@ -75,6 +77,7 @@
     pool_sem,
     line_sem,
     query_sem,
+    row_sem,
 ):
     slots, block_width = k_vm.shape[0], k_vm.shape[1]
     requests = q_all.shape[0]
@@ -122,16 +125,15 @@
 
     pl.semaphore_wait(barrier, len(LINE_Z) + len(LINE_X) + len(pool_peers))
 
-    def to_group(src, dst, phase, half):
-        for peer in peers:
-            pltpu.make_async_remote_copy(
-                src_ref=src(peer),
-                dst_ref=dst,
-                send_sem=send_sem.at[phase, half],
-                recv_sem=recv_sem.at[phase, half],
-                device_id={"group": peer},
-                device_id_type=MESH,
-            ).start()
+    def send(src, dst, peer, phase, half):
+        pltpu.make_async_remote_copy(
+            src_ref=src,
+            dst_ref=dst,
+            send_sem=send_sem.at[phase, half],
+            recv_sem=recv_sem.at[phase, half],
+            device_id={"group": peer},
+            device_id_type=MESH,
+        ).start()
 
     def send_query(owner, target, sem):
         pltpu.make_async_remote_copy(
@@ -256,8 +258,9 @@
             )
         table[half] = table_f32[...].astype(jnp.bfloat16).reshape(requests, ROWS, HD)
 
-        to_group(lambda peer: stats.at[half, peer], got_stats.at[half, g], 0, half)
-        to_group(lambda peer: table.at[half, peer], got.at[half, g], 1, half)
+        for peer in peers:
+            send(stats.at[half, peer], got_stats.at[half, g], peer, 0, half)
+            send(table.at[half, peer], got.at[half, g], peer, 1, half)
         got[half, g] = table[half, g]
         got_stats[half, g] = stats[half, g]
 
@@ -286,33 +289,43 @@
             attention += held_scale[:, h : h + 1] * got[half, h].astype(jnp.float32)
         att_all[half, g] = attention.astype(jnp.bfloat16)
         mine = att_all.at[half, g]
-        to_group(lambda peer: mine, mine, 2, half)
+        for dz, dx in ROWS_NEAR:
+            pltpu.make_async_remote_copy(
+                src_ref=mine,
+                dst_ref=mine,
+                send_sem=send_sem.at[2, half],
+                recv_sem=row_sem.at[half, dz],
+                device_id={"group": peer_at(dz, dx)},
+                device_id_type=MESH,
+            ).start()
 
     loads[2].wait()
-    y = jnp.zeros((requests * STEPS, w_vm.shape[1]), jnp.float32)
-    for half in range(HALVES):
-        wait_bytes(att_all.at[half, others], recv_sem.at[2, half])
-        att_f32[...] = att_all[half].reshape(requests * ROWS, HD).astype(jnp.float32)
-        att = jnp.concatenate(
-            [
-                att_f32[pl.ds(h, requests * STEPS, stride=HEADS), :].astype(jnp.bfloat16)
-                for h in range(HEADS)
-            ],
-            axis=1,
-        )
-        rows = pl.ds(half * HEADS * HD, HEADS * HD)
-        y += jnp.dot(att, w_vm[rows, :], preferred_element_type=jnp.float32)
-    y_f32[...] = y.reshape(y_f32.shape)
-
-    for peer in pool_peers:
-        pltpu.make_async_remote_copy(
-            src_ref=y_f32.at[peer],
-            dst_ref=y_got.at[p],
-            send_sem=pool_sem.at[0],
-            recv_sem=pool_sem.at[1],
-            device_id={"pool": peer},
-            device_id_type=MESH,
-        ).start()
+    for dz in ROW_ORDER:
+        block = lax.rem(z + NZ - dz, NZ)
+        arriving = NX if dz else NX - 1
+        members = pl.ds(pl.multiple_of(block * NX, NX), NX)
+        heads = []
+        for half in range(HALVES):
+            wait_bytes(att_all.at[half, pl.ds(0, arriving)], row_sem.at[half, dz])
+            att_f32[half] = att_all[half, members].reshape(NX * ROWS, HD).astype(jnp.float32)
+            for h in range(HEADS):
+                head = att_f32[half, pl.ds(h, NX * STEPS, stride=HEADS), :]
+                heads.append(head.astype(jnp.bfloat16))
+        y_f32[block] = jnp.dot(
+            jnp.concatenate(heads, axis=1), w_vm[...], preferred_element_type=jnp.float32
+        )
+
+        @pl.when(block != p)
+        def _():
+            pltpu.make_async_remote_copy(
+                src_ref=y_f32.at[block],
+                dst_ref=y_got.at[p],
+                send_sem=pool_sem.at[0],
+                recv_sem=pool_sem.at[1],
+                device_id={"pool": block},
+                device_id_type=MESH,
+            ).start()
+
     wait_bytes(y_got.at[pl.ds(0, pools - 1)], pool_sem.at[1])
     result = y_f32[p]
     for peer in pool_peers:
@@ -367,7 +380,7 @@
             pltpu.VMEM((HALVES, requests, ROWS, HD), jnp.bfloat16),
             pltpu.VMEM((HALVES, requests, 1, HD), jnp.float32),
             pltpu.VMEM((HALVES, requests, ROWS, HD), jnp.bfloat16),
-            pltpu.VMEM((requests * ROWS, HD), jnp.float32),
+            pltpu.VMEM((HALVES, NX * ROWS, HD), jnp.float32),
             pltpu.VMEM((pools, out_rows, columns), jnp.float32),
             pltpu.VMEM((pools, out_rows, columns), jnp.float32),
             pltpu.VMEM(queries.shape, jnp.bfloat16),
@@ -382,6 +395,7 @@
             pltpu.SemaphoreType.DMA((2,)),
             pltpu.SemaphoreType.DMA((NZ,)),
             pltpu.SemaphoreType.DMA((2,)),
+            pltpu.SemaphoreType.DMA((HALVES, NZ)),
         ],
         compiler_params=pltpu.CompilerParams(
             collective_id=0, has_side_effects=True, vmem_limit_bytes=48 << 20

time: 40.3 us -> 38.8 us (0.963)
  Pallas kernels: 39.6 us -> 38.1 us
    pallas_call x1, Pallas kernels: 39.6 us -> 38.1 us  [body(): pl.pallas_call(kernel, out_shape=jax.ShapeDtypeStruct((out_rows, columns)...]
where the time goes in v4:
time: 38.8 us; the launch traced here: 38.7 us
  Pallas kernels  38.1 us (98%)
  local copies, waits for them, and re-layouts  0.6 us (2%)
    pallas_call x1, Pallas kernels, body(): pl.pallas_call(kernel, out_shape=jax.ShapeDtypeStruct((out_rows, columns)...  38.1 us

profile of v4, /device:TPU:1, one launch (start us, length us, event | category | flops | bytes accessed | tf_op | source)
XLA Modules:
  0.0 38.7 jit_solution(3254191152782242770)
XLA Ops:
  0.0 38.1 %paged_attention.1 = bf16[16,256]{1,0:T(8,128)(2,1)S(1)} custom-call(bf16[1,4,1024]{2,1,0:T(4,128)(2,1)} %q_hbm.1, bf16[1,4,128]{2,1,0:T(4,128)(2,1)} %nk_hbm.1, bf16[1,4,128]{2,1,0:T(4,128)(2,1)} %nv_hbm.1, s32[32]{0:T(128)} %len_hbm.1, s32[32]{0:T(128)} %sreq_hbm.1, s32[32]{0:T(128)} %sblk_hbm.1, bf16[32,512,128]{2,1,0:T(8,128)(2,1)} %k_hbm.1, ...), custom_call_target="tpu_custom_call" | custom-call | tf_op jit(solution)/shard_map/paged_attention/pallas_call | solution.py:362
  38.1 0.6 %copy.11 = bf16[16,256]{1,0:T(8,128)(2,1)} copy(bf16[16,256]{1,0:T(8,128)(2,1)S(1)} %paged_attention.1) | data formatting | bytes 16384

commit v5 on v4

--- a/solution.py
+++ b/solution.py
@@ -24,7 +24,7 @@
 LINE_Z = (4, 3, 5, 2, 6, 1, 7)
 LINE_X = (2, 1, 3)
 ROWS_NEAR = EVERY[::-1]
-ROW_ORDER = (0, 1, 7, 2, 6, 3, 5, 4)
+ROW_ORDER = (0, 7, 1, 6, 2, 5, 3, 4)
 
 MESH = pl.DeviceIdType.MESH
 masked_score = -1e30

time: 38.8 us -> 38 us (0.979)
  Pallas kernels: 38.1 us -> 37.3 us
    pallas_call x1, Pallas kernels: 38.1 us -> 37.3 us  [body(): pl.pallas_call(kernel, out_shape=jax.ShapeDtypeStruct((out_rows, columns)...]
where the time goes in v5:
time: 38 us; the launch traced here: 37.9 us
  Pallas kernels  37.3 us (98%)
  local copies, waits for them, and re-layouts  0.6 us (2%)
    pallas_call x1, Pallas kernels, body(): pl.pallas_call(kernel, out_shape=jax.ShapeDtypeStruct((out_rows, columns)...  37.3 us

profile of v5, /device:TPU:1, one launch (start us, length us, event | category | flops | bytes accessed | tf_op | source)
XLA Modules:
  0.0 37.9 jit_solution(387735232426163267)
XLA Ops:
  0.0 37.3 %paged_attention.1 = bf16[16,256]{1,0:T(8,128)(2,1)S(1)} custom-call(bf16[1,4,1024]{2,1,0:T(4,128)(2,1)} %q_hbm.1, bf16[1,4,128]{2,1,0:T(4,128)(2,1)} %nk_hbm.1, bf16[1,4,128]{2,1,0:T(4,128)(2,1)} %nv_hbm.1, s32[32]{0:T(128)} %len_hbm.1, s32[32]{0:T(128)} %sreq_hbm.1, s32[32]{0:T(128)} %sblk_hbm.1, bf16[32,512,128]{2,1,0:T(8,128)(2,1)} %k_hbm.1, ...), custom_call_target="tpu_custom_call" | custom-call | tf_op jit(solution)/shard_map/paged_attention/pallas_call | solution.py:362
  37.3 0.6 %copy.11 = bf16[16,256]{1,0:T(8,128)(2,1)} copy(bf16[16,256]{1,0:T(8,128)(2,1)S(1)} %paged_attention.1) | data formatting | bytes 16384
